TPU v7x, 32 devices: a whole 2x2x4 slice. The times are simulated.
32 devices in a mesh: blk: 16 (over z, y, x), layer: 2 (over core).
Axes of the slice: x: 2, y: 2, z: 4, core: 2. Of those that a mesh axis runs over, the one named last changes fastest.
Arguments:
- train_factors: bfloat16 [192, 2, 2, 64, 1024], P('blk', 'layer'), may hold values from -0.29882812 to 0.29882812
- val_factors: bfloat16 [64, 2, 2, 64, 1024], P('blk', 'layer'), may hold values from -0.29882812 to 0.29882812
Outputs:
- scores: float32 [192, 3, 4], P('blk')
All inputs are finite; a program needn't handle non-finite values.
Results may differ from a plain program's by a relative error of at most 0.0003.
Values may be sent and summed in bfloat16 or wider, within the bound.
No kernel may reach another device: no remote copies, remote signals or barrier semaphores. Data moves between devices by JAX's collectives and lax.ppermute only.
A program may use at most 64 MiB of HBM per device.

v0:
```python
import functools

import jax
import jax.numpy as jnp
from jax import lax
from jax.experimental import pallas as pl
from jax.experimental.pallas import tpu as pltpu
from jax.sharding import PartitionSpec as P

CUTS = 4
GROUP = 4

VMEM = pl.BlockSpec(memory_space=pltpu.VMEM)


def permuted(block, axis, target):
    size = lax.axis_size(axis)
    return lax.ppermute(block, axis, [(i, target(i) % size) for i in range(size)])


def call(kernel, out_shape, specs, operands, flops=0, scratch=(), vmem=16 << 20):
    shapes = list(operands) + jax.tree.leaves(out_shape)
    return pl.pallas_call(
        kernel,
        out_shape=out_shape,
        in_specs=specs,
        out_specs=jax.tree.map(lambda _: VMEM, out_shape),
        scratch_shapes=scratch,
        compiler_params=pltpu.CompilerParams(vmem_limit_bytes=vmem),
        cost_estimate=pl.CostEstimate(
            flops=flops,
            bytes_accessed=sum(x.size * x.dtype.itemsize for x in shapes),
            transcendentals=0,
        ),
    )(*operands)


def groups(train_ref):
    examples = train_ref.shape[0]
    size = GROUP if examples % GROUP == 0 else 1
    return [slice(first, first + size) for first in range(0, examples, size)]


def gram(train_ref, val_refs, layer, index, group, start=0):
    total = 0.0
    for ref in val_refs:
        depth = ref.shape[-1]
        train = train_ref[group, layer, index, :, start : start + depth].reshape(-1, depth)
        val = ref[:, layer, index].reshape(-1, depth)
        total = total + lax.dot_general(
            train, val, (((1,), (1,)), ((), ())), preferred_element_type=jnp.float32
        )
        start += depth
    return total


def token_sums(product, tokens):
    return jnp.sum(product.reshape(-1, tokens, product.shape[-1]), axis=1)


def example_sums(by_token, tokens):
    count = by_token.shape[-1] // tokens
    shape = (count, by_token.shape[-1])
    token = lax.broadcasted_iota(jnp.int32, shape, 1) // tokens
    mine = (token == lax.broadcasted_iota(jnp.int32, shape, 0)).astype(jnp.bfloat16)
    total, rest = 0.0, by_token
    for _ in range(3):
        piece = rest.astype(jnp.bfloat16)
        rest = rest - piece.astype(jnp.float32)
        total = total + lax.dot_general(
            mine, piece, (((1,), (1,)), ((), ())), preferred_element_type=jnp.float32
        )
    return total


def scores(train_ref, val_refs):
    layers, tokens = train_ref.shape[1], train_ref.shape[3]
    sums = []
    for group in groups(train_ref):
        product = 0.0
        for layer in range(layers):
            product = product + gram(train_ref, val_refs, layer, 0, group) * gram(
                train_ref, val_refs, layer, 1, group
            )
        sums.append(token_sums(product, tokens))
    return example_sums(jnp.concatenate(sums, axis=0), tokens)


def cut_kernel(val_ref, *part_refs):
    for c, ref in enumerate(part_refs, 1):
        depth = ref.shape[-1]
        ref[...] = val_ref[..., c * depth : (c + 1) * depth]


def scores_kernel(train_ref, *refs):
    *val_refs, out_ref = refs
    out_ref[...] = scores(train_ref, val_refs)


def by_parity(even, odd):
    parity = lax.rem(lax.axis_index("blk"), 2)
    pl.when(parity == 0)(even)
    pl.when(parity == 1)(odd)


def pick_kernel(even_ref, odd_ref, *refs):
    out_ref = refs[-1]

    def put(ref):
        out_ref[...] = ref[...]

    by_parity(lambda: put(even_ref), lambda: put(odd_ref))


def pick_last_kernel(even_ref, odd_ref, *refs):
    out_ref = refs[-1]
    count = out_ref.shape[0]

    def put(ref):
        out_ref[...] = ref[ref.shape[0] - count :]

    by_parity(lambda: put(even_ref), lambda: put(odd_ref))


def columns(first, count, tokens):
    return slice(first * tokens, (first + count) * tokens)


def grams_kernel(train_ref, *refs):
    *part_refs, out_ref = refs
    layers, tokens = train_ref.shape[1], train_ref.shape[3]
    for layer in range(layers):
        for index in range(2):
            for group in groups(train_ref):
                rows = slice(group.start * tokens, group.stop * tokens)
                out_ref[layer, index, rows] = gram(train_ref, part_refs, layer, index, group)


def second_kernel(train_ref, part_ref, grams_ref, out_ref):
    layers, tokens, features = train_ref.shape[1], train_ref.shape[3], train_ref.shape[4]
    start = features - part_ref.shape[-1]
    sums = []
    for group in groups(train_ref):
        rows = slice(group.start * tokens, group.stop * tokens)
        product = 0.0
        for layer in range(layers):
            act, grad = (
                grams_ref[layer, index, rows] + gram(train_ref, [part_ref], layer, index, group, start)
                for index in range(2)
            )
            product = product + act * grad
        sums.append(token_sums(product, tokens))
    out_ref[...] = example_sums(jnp.concatenate(sums, axis=0), tokens)


def middle_kernel(train_ref, part_ref, last_ref, grams_ref, ends_ref, out_ref):
    layers, tokens, features = train_ref.shape[1], train_ref.shape[3], train_ref.shape[4]
    depth = part_ref.shape[-1]
    detour = columns(0, out_ref.shape[0], tokens)
    rest = slice(detour.stop, grams_ref.shape[-1])
    sums = []
    for group in groups(train_ref):
        rows = slice(group.start * tokens, group.stop * tokens)
        product = 0.0
        for layer in range(layers):
            totals = [
                grams_ref[layer, index, rows]
                + gram(train_ref, [part_ref], layer, index, group, features - 2 * depth)
                for index in range(2)
            ]
            act, grad = (
                totals[index][:, detour]
                + gram(train_ref, [last_ref], layer, index, group, features - depth)
                for index in range(2)
            )
            product = product + act * grad
            for index in range(2):
                ends_ref[layer, index, rows] = totals[index][:, rest]
        sums.append(token_sums(product, tokens))
    out_ref[...] = example_sums(jnp.concatenate(sums, axis=0), tokens)


def last_kernel(train_ref, end_ref, ends_ref, own_ref, first_ref, second_ref, out_ref):
    layers, tokens, features = train_ref.shape[1], train_ref.shape[3], train_ref.shape[4]
    start = features - end_ref.shape[-1]
    sums = []
    for group in groups(train_ref):
        rows = slice(group.start * tokens, group.stop * tokens)
        product = 0.0
        for layer in range(layers):
            act, grad = (
                ends_ref[layer, index, rows] + gram(train_ref, [end_ref], layer, index, group, start)
                for index in range(2)
            )
            product = product + act * grad
        sums.append(token_sums(product, tokens))
    ready = first_ref.shape[0]
    out_ref[0] = own_ref[...]
    out_ref[1, :ready] = first_ref[...]
    out_ref[1, ready:] = example_sums(jnp.concatenate(sums, axis=0), tokens)
    out_ref[2] = second_ref[...]


def summed(rows, axis):
    if lax.axis_size(axis) != 2:
        return lax.psum(rows, axis)
    return rows + permuted(rows, axis, lambda i: i ^ 1)


def local(train, val):
    examples, layers, _, tokens, features = train.shape
    count = val.shape[0]
    cuts = CUTS
    depth = features // cuts
    work = 4 * examples * count * layers * tokens * tokens * features
    part = jax.ShapeDtypeStruct(val.shape[:-1] + (depth,), val.dtype)
    small = jax.ShapeDtypeStruct((1,) + part.shape[1:], val.dtype)
    rows = jax.ShapeDtypeStruct((count, examples), jnp.float32)
    grams = jax.ShapeDtypeStruct((layers, 2, examples * tokens, count * tokens), jnp.float32)

    detour = val[: count - 1, ..., (cuts - 1) * depth :]
    parts = [val[..., :depth], *call(cut_kernel, [part] * (cuts - 1), [VMEM], [val])]
    second = [permuted(x, "blk", lambda i: i + 2) for x in parts]
    near_last = permuted(detour, "blk", lambda i: i ^ 1)
    far_last = permuted(near_last, "blk", lambda i: i + 2)
    first = []
    for c in range(cuts - 1):
        operands = [parts[c], second[c]] + ([near_last] if c == 1 else [])
        picked = call(pick_kernel, part, [VMEM] * len(operands), operands)
        first.append(permuted(picked, "blk", lambda i: i ^ 1))
    sums = call(grams_kernel, grams, [VMEM] * (cuts - 1), [train] + first[:-1], work // 2)
    far = call(grams_kernel, grams, [VMEM] * cuts, [train] + second[:-1], work)
    operands = [parts[-1], second[-1], far]
    picked = call(pick_last_kernel, small, [VMEM] * len(operands), operands)
    end = permuted(picked, "blk", lambda i: i ^ 1)

    own = call(scores_kernel, rows, [VMEM] * (1 + cuts), [train] + parts, work)
    far = call(second_kernel, rows, [VMEM] * 3, [train, second[-1], far], work // 4)
    last = call(pick_kernel, detour, [VMEM] * 3, [far_last, near_last, sums], work)
    ends = jax.ShapeDtypeStruct(grams.shape[:-1] + (tokens,), jnp.float32)
    ready = jax.ShapeDtypeStruct((count - 1, examples), jnp.float32)
    operands = [train, first[-1], last, sums]
    ends, ready = call(middle_kernel, [ends, ready], [VMEM] * len(operands), operands, work // 4)
    out = jax.ShapeDtypeStruct((3,) + rows.shape, jnp.float32)
    operands = [train, end, ends, own, ready, far]
    partial_rows = call(last_kernel, out, [VMEM] * len(operands), operands, work // 16)
    return summed(partial_rows, "layer").transpose(2, 0, 1)


def solution(mesh):
    return jax.shard_map(
        local,
        mesh=mesh,
        in_specs=(P("blk", "layer", None, None, None), P("blk", "layer", None, None, None)),
        out_specs=P("blk", None, None),
        check_vma=False,
    )
```

profile of v0, /device:TPU:0, one launch (start us, length us, event | category | flops | bytes accessed | tf_op | source)
XLA Modules:
  0.0 37.5 jit_solution(10896419191466338290)
XLA Ops:
  0.0 1.0 %slice.6.even_ref.refs_0_ = bf16[4,1,2,64,256]{4,3,2,1,0:T(8,128)(2,1)S(1)} slice(bf16[4,1,2,64,1024]{4,3,2,1,0:T(8,128)(2,1)} %val_ref.1), slice={[0:4], [0:1], [0:2], [0:64], [0:256]} | slice | bytes 524288 | tf_op jit(solution)/shard_map/slice | solution.py:222
  1.0 3.0 %collective-permute-start.1 = (bf16[4,1,2,64,256]{4,3,2,1,0:T(8,128)(2,1)S(1)}, bf16[4,1,2,64,256]{4,3,2,1,0:T(8,128)(2,1)S(1)}, u32[]{:S(2)}, u32[]{:S(2)}) collective-permute-start(bf16[4,1,2,64,256]{4,3,2,1,0:T(8,128)(2,1)S(1)} %slice.6.even_ref.refs_0_), channel_id=1, source_target_pairs={{0,4},{2,6},{4,8},{6,10},{8,12},{10,14},{12,16},{14,18},{16,20},{1... | collective-permute-start | bytes 786440 | tf_op jit(solution)/shard_map/ppermute | solution.py:18
  4.0 0.0 copy-start.1
  4.0 1.2 %copy-done.1 = bf16[4,1,2,64,1024]{4,3,2,1,0:T(8,128)(2,1)S(1)} copy-done((bf16[4,1,2,64,1024]{4,3,2,1,0:T(8,128)(2,1)S(1)}, bf16[4,1,2,64,1024]{4,3,2,1,0:T(8,128)(2,1)}, u32[]{:S(2)}) %copy-start.1) | copy-done | bytes 1048600
  5.2 0.0 copy-start
  5.2 0.1 shard_map.28
  5.3 1.6 %collective-permute-start.2 = (bf16[4,1,2,64,256]{4,3,2,1,0:T(8,128)(2,1)S(1)}, bf16[4,1,2,64,256]{4,3,2,1,0:T(8,128)(2,1)S(1)}, u32[]{:S(2)}, u32[]{:S(2)}) collective-permute-start(bf16[4,1,2,64,256]{4,3,2,1,0:T(8,128)(2,1)S(1)} %get-tuple-element.11.even_ref.refs_1_), channel_id=1, source_target_pairs={{0,4},{2,6},{4,8},{6,10},{8,12},{10,14},{12,16},{14,18},{16,20},{1... | collective-permute-start | bytes 786440 | tf_op jit(solution)/shard_map/ppermute | solution.py:18
  6.9 1.6 %collective-permute-start.6 = (bf16[3,1,2,64,256]{4,3,2,1,0:T(8,128)(2,1)S(1)}, bf16[3,1,2,64,256]{4,3,2,1,0:T(8,128)(2,1)S(1)}, u32[]{:S(2)}, u32[]{:S(2)}) collective-permute-start(bf16[3,1,2,64,256]{4,3,2,1,0:T(8,128)(2,1)S(1)} %slice.7), channel_id=1, source_target_pairs={{0,2},{2,0},{4,6},{6,4},{8,10},{10,8},{12,14},{14,12},{16,18},{18,... | collective-permute-start | bytes 589832 | tf_op jit(solution)/shard_map/ppermute | solution.py:18
  8.4 1.5 %collective-permute-start.3 = (bf16[4,1,2,64,256]{4,3,2,1,0:T(8,128)(2,1)S(1)}, bf16[4,1,2,64,256]{4,3,2,1,0:T(8,128)(2,1)S(1)}, u32[]{:S(2)}, u32[]{:S(2)}) collective-permute-start(bf16[4,1,2,64,256]{4,3,2,1,0:T(8,128)(2,1)S(1)} %get-tuple-element.12.even_ref.refs_2_), channel_id=1, source_target_pairs={{0,4},{2,6},{4,8},{6,10},{8,12},{10,14},{12,16},{14,18},{16,20},{1... | collective-permute-start | bytes 786440 | tf_op jit(solution)/shard_map/ppermute | solution.py:18
  10.0 1.5 %collective-permute-start = (bf16[4,1,2,64,256]{4,3,2,1,0:T(8,128)(2,1)S(1)}, bf16[4,1,2,64,256]{4,3,2,1,0:T(8,128)(2,1)S(1)}, u32[]{:S(2)}, u32[]{:S(2)}) collective-permute-start(bf16[4,1,2,64,256]{4,3,2,1,0:T(8,128)(2,1)S(1)} %get-tuple-element.10.even_ref.refs_3_), channel_id=1, source_target_pairs={{0,4},{2,6},{4,8},{6,10},{8,12},{10,14},{12,16},{14,18},{16,20},{1... | collective-permute-start | bytes 786440 | tf_op jit(solution)/shard_map/ppermute | solution.py:18
  11.5 2.7 %collective-permute-done.1.refs_0_.odd_ref = bf16[4,1,2,64,256]{4,3,2,1,0:T(8,128)(2,1)S(1)} collective-permute-done((bf16[4,1,2,64,256]{4,3,2,1,0:T(8,128)(2,1)S(1)}, bf16[4,1,2,64,256]{4,3,2,1,0:T(8,128)(2,1)S(1)}, u32[]{:S(2)}, u32[]{:S(2)}) %collective-permute-start.1) | collective-permute-done | bytes 262176 | tf_op jit(solution)/shard_map/ppermute | solution.py:18
  14.2 1.7 %collective-permute-start.8 = (bf16[4,1,2,64,256]{4,3,2,1,0:T(8,128)(2,1)S(1)}, bf16[4,1,2,64,256]{4,3,2,1,0:T(8,128)(2,1)S(1)}, u32[]{:S(2)}, u32[]{:S(2)}) collective-permute-start(bf16[4,1,2,64,256]{4,3,2,1,0:T(8,128)(2,1)S(1)} %shard_map.32), channel_id=1, source_target_pairs={{0,2},{2,0},{4,6},{6,4},{8,10},{10,8},{12,14},{14,12},{16,18},{18,... | collective-permute-start | bytes 786440 | tf_op jit(solution)/shard_map/ppermute | solution.py:18
  15.9 0.0 collective-permute-done.6.refs_0_.odd_ref
  15.9 3.9 %collective-permute-done.2.refs_1_.odd_ref = bf16[4,1,2,64,256]{4,3,2,1,0:T(8,128)(2,1)S(1)} collective-permute-done((bf16[4,1,2,64,256]{4,3,2,1,0:T(8,128)(2,1)S(1)}, bf16[4,1,2,64,256]{4,3,2,1,0:T(8,128)(2,1)S(1)}, u32[]{:S(2)}, u32[]{:S(2)}) %collective-permute-start.2) | collective-permute-done | bytes 262176 | tf_op jit(solution)/shard_map/ppermute | solution.py:18
  19.8 1.7 %collective-permute-start.9 = (bf16[4,1,2,64,256]{4,3,2,1,0:T(8,128)(2,1)S(1)}, bf16[4,1,2,64,256]{4,3,2,1,0:T(8,128)(2,1)S(1)}, u32[]{:S(2)}, u32[]{:S(2)}) collective-permute-start(bf16[4,1,2,64,256]{4,3,2,1,0:T(8,128)(2,1)S(1)} %shard_map.33), channel_id=1, source_target_pairs={{0,2},{2,0},{4,6},{6,4},{8,10},{10,8},{12,14},{14,12},{16,18},{18,... | collective-permute-start | bytes 786440 | tf_op jit(solution)/shard_map/ppermute | solution.py:18
  21.5 0.0 collective-permute-start.7
  21.5 3.9 %collective-permute-done.3.refs_2_.odd_ref = bf16[4,1,2,64,256]{4,3,2,1,0:T(8,128)(2,1)S(1)} collective-permute-done((bf16[4,1,2,64,256]{4,3,2,1,0:T(8,128)(2,1)S(1)}, bf16[4,1,2,64,256]{4,3,2,1,0:T(8,128)(2,1)S(1)}, u32[]{:S(2)}, u32[]{:S(2)}) %collective-permute-start.3) | collective-permute-done | bytes 262176 | tf_op jit(solution)/shard_map/ppermute | solution.py:18
  25.4 1.7 %collective-permute-start.5 = (bf16[4,1,2,64,256]{4,3,2,1,0:T(8,128)(2,1)S(1)}, bf16[4,1,2,64,256]{4,3,2,1,0:T(8,128)(2,1)S(1)}, u32[]{:S(2)}, u32[]{:S(2)}) collective-permute-start(bf16[4,1,2,64,256]{4,3,2,1,0:T(8,128)(2,1)S(1)} %shard_map.31), channel_id=1, source_target_pairs={{0,2},{2,0},{4,6},{6,4},{8,10},{10,8},{12,14},{14,12},{16,18},{18,... | collective-permute-start | bytes 786440 | tf_op jit(solution)/shard_map/ppermute | solution.py:18
  27.2 0.0 copy-done
  27.2 1.1 %shard_map.37.own_ref = f32[4,12]{1,0:T(4,128)S(1)} custom-call(bf16[12,1,2,64,1024]{4,3,2,1,0:T(8,128)(2,1)S(1)} %copy-done, bf16[4,1,2,64,256]{4,3,2,1,0:T(8,128)(2,1)S(1)} %slice.6.even_ref.refs_0_, bf16[4,1,2,64,256]{4,3,2,1,0:T(8,128)(2,1)S(1)} %get-tuple-element.11.even_ref.refs_1_, bf16[4,1,2,64,256]{4,3,2,1,0:T(8,128)(2,1)S(1)} %get-tuple-element.12.even_ref.refs_2_, ...), custom_call_target="tpu_custom_call" | custom-call | flops 805306368 | bytes 4194496 | tf_op jit(solution)/shard_map/pallas_call | solution.py:23
  28.3 0.8 %shard_map.29.refs_0_.grams_ref = f32[1,2,768,256]{3,2,1,0:T(8,128)S(1)} custom-call(bf16[12,1,2,64,1024]{4,3,2,1,0:T(8,128)(2,1)S(1)} %copy-done, bf16[4,1,2,64,256]{4,3,2,1,0:T(8,128)(2,1)S(1)} %collective-permute-done.1.refs_0_.odd_ref, bf16[4,1,2,64,256]{4,3,2,1,0:T(8,128)(2,1)S(1)} %collective-permute-done.2.refs_1_.odd_ref, ...), custom_call_target="tpu_custom_call" | custom-call | flops 805306368 | bytes 5505024 | tf_op jit(solution)/shard_map/pallas_call | solution.py:23
  29.1 1.9 %collective-permute-done.odd_ref.part_ref = bf16[4,1,2,64,256]{4,3,2,1,0:T(8,128)(2,1)S(1)} collective-permute-done((bf16[4,1,2,64,256]{4,3,2,1,0:T(8,128)(2,1)S(1)}, bf16[4,1,2,64,256]{4,3,2,1,0:T(8,128)(2,1)S(1)}, u32[]{:S(2)}, u32[]{:S(2)}) %collective-permute-start) | collective-permute-done | bytes 262176 | tf_op jit(solution)/shard_map/ppermute | solution.py:18
  31.0 1.7 %collective-permute-start.4 = (bf16[1,1,2,64,256]{4,3,2,1,0:T(8,128)(2,1)S(1)}, bf16[1,1,2,64,256]{4,3,2,1,0:T(8,128)(2,1)S(1)}, u32[]{:S(2)}, u32[]{:S(2)}) collective-permute-start(bf16[1,1,2,64,256]{4,3,2,1,0:T(8,128)(2,1)S(1)} %shard_map.30), channel_id=1, source_target_pairs={{0,2},{2,0},{4,6},{6,4},{8,10},{10,8},{12,14},{14,12},{16,18},{18,... | collective-permute-start | bytes 196616 | tf_op jit(solution)/shard_map/ppermute | solution.py:18
  32.7 0.5 %shard_map.38.second_ref = f32[4,12]{1,0:T(4,128)S(1)} custom-call(bf16[12,1,2,64,1024]{4,3,2,1,0:T(8,128)(2,1)S(1)} %copy-done, bf16[4,1,2,64,256]{4,3,2,1,0:T(8,128)(2,1)S(1)} %collective-permute-done.odd_ref.part_ref, f32[1,2,768,256]{3,2,1,0:T(8,128)S(1)} %shard_map.29.refs_0_.grams_ref), custom_call_target="tpu_custom_call" | custom-call | flops 201326592 | bytes 4980928 | tf_op jit(solution)/shard_map/pallas_call | solution.py:23
  33.2 0.0 collective-permute-done.8.refs_0_
  33.2 0.0 collective-permute-done.9.refs_1_
  33.3 0.6 %shard_map.34.refs_0_.grams_ref = f32[1,2,768,256]{3,2,1,0:T(8,128)S(1)} custom-call(bf16[12,1,2,64,1024]{4,3,2,1,0:T(8,128)(2,1)S(1)} %copy-done, bf16[4,1,2,64,256]{4,3,2,1,0:T(8,128)(2,1)S(1)} %collective-permute-done.8.refs_0_, bf16[4,1,2,64,256]{4,3,2,1,0:T(8,128)(2,1)S(1)} %collective-permute-done.9.refs_1_), custom_call_target="tpu_custom_call" | custom-call | flops 402653184 | bytes 5242880 | tf_op jit(solution)/shard_map/pallas_call | solution.py:23
  33.9 0.5 %collective-permute-done.7.even_ref = bf16[3,1,2,64,256]{4,3,2,1,0:T(8,128)(2,1)S(1)} collective-permute-done((bf16[3,1,2,64,256]{4,3,2,1,0:T(8,128)(2,1)S(1)}, bf16[3,1,2,64,256]{4,3,2,1,0:T(8,128)(2,1)S(1)}, u32[]{:S(2)}, u32[]{:S(2)}) %collective-permute-start.7) | collective-permute-done | bytes 196640 | tf_op jit(solution)/shard_map/ppermute | solution.py:18
  34.4 0.0 collective-permute-done.5.part_ref
  34.4 0.8 %shard_map.36 = (f32[1,2,768,64]{3,2,1,0:T(8,128)S(1)}, f32[3,12]{1,0:T(4,128)S(1)}) custom-call(bf16[12,1,2,64,1024]{4,3,2,1,0:T(8,128)(2,1)S(1)} %copy-done, bf16[4,1,2,64,256]{4,3,2,1,0:T(8,128)(2,1)S(1)} %collective-permute-done.5.part_ref, bf16[3,1,2,64,256]{4,3,2,1,0:T(8,128)(2,1)S(1)} %shard_map.35.last_ref, ...), custom_call_target="tpu_custom_call" | custom-call | flops 201326592 | bytes 5570704 | tf_op jit(solution)/shard_map/pallas_call | solution.py:23
  35.2 0.1 collective-permute-done.4.end_ref
  35.3 0.5 %shard_map.39 = f32[3,4,12]{2,1,0:T(4,128)S(1)} custom-call(bf16[12,1,2,64,1024]{4,3,2,1,0:T(8,128)(2,1)S(1)} %copy-done, bf16[1,1,2,64,256]{4,3,2,1,0:T(8,128)(2,1)S(1)} %collective-permute-done.4.end_ref, f32[1,2,768,64]{3,2,1,0:T(8,128)S(1)} %get-tuple-element.13.ends_ref, f32[4,12]{1,0:T(4,128)S(1)} %shard_map.37.own_ref, ...), custom_call_target="tpu_custom_call" | custom-call | flops 50331648 | bytes 3605584 | tf_op jit(solution)/shard_map/pallas_call | solution.py:23
  35.8 0.0 collective-permute-start.10
  35.8 1.2 %collective-permute-done.10 = f32[3,4,12]{2,1,0:T(4,128)S(1)} collective-permute-done((f32[3,4,12]{2,1,0:T(4,128)S(1)}, f32[3,4,12]{2,1,0:T(4,128)S(1)}, u32[]{:S(2)}, u32[]{:S(2)}) %collective-permute-start.10) | collective-permute-done | bytes 608 | tf_op jit(solution)/shard_map/ppermute | solution.py:18
  37.0 0.6 %add_bitcast_fusion = f32[12,3,4]{0,2,1:T(4,128)} fusion(f32[3,4,12]{2,1,0:T(4,128)S(1)} %shard_map.39, f32[3,4,12]{2,1,0:T(4,128)S(1)} %collective-permute-done.10), kind=kLoop, calls=%fused_computation | loop fusion | flops 144 | bytes 1728 | tf_op jit(solution)/shard_map/transpose | solution.py:247
  (6 shorter events, 0.1 us)
Async XLA Ops:
  1.0 13.2 %collective-permute-start.1 = (bf16[4,1,2,64,256]{4,3,2,1,0:T(8,128)(2,1)S(1)}, bf16[4,1,2,64,256]{4,3,2,1,0:T(8,128)(2,1)S(1)}, u32[]{:S(2)}, u32[]{:S(2)}) collective-permute-start(bf16[4,1,2,64,256]{4,3,2,1,0:T(8,128)(2,1)S(1)} %slice.6.even_ref.refs_0_), channel_id=1, source_target_pairs={{0,4},{2,6},{4,8},{6,10},{8,12},{10,14},{12,16},{14,18},{16,20},{1... | collective-permute-start | bytes 786440 | tf_op jit(solution)/shard_map/ppermute | solution.py:18
  4.0 1.2 %copy-start.1 = (bf16[4,1,2,64,1024]{4,3,2,1,0:T(8,128)(2,1)S(1)}, bf16[4,1,2,64,1024]{4,3,2,1,0:T(8,128)(2,1)}, u32[]{:S(2)}) copy-start(bf16[4,1,2,64,1024]{4,3,2,1,0:T(8,128)(2,1)} %val_ref.1) | copy-start | bytes 3145732
  5.2 21.9 %copy-start = (bf16[12,1,2,64,1024]{4,3,2,1,0:T(8,128)(2,1)S(1)}, bf16[12,1,2,64,1024]{4,3,2,1,0:T(8,128)(2,1)}, u32[]{:S(2)}) copy-start(bf16[12,1,2,64,1024]{4,3,2,1,0:T(8,128)(2,1)} %train_ref.11) | copy-start | bytes 9437188
  5.3 14.5 %collective-permute-start.2 = (bf16[4,1,2,64,256]{4,3,2,1,0:T(8,128)(2,1)S(1)}, bf16[4,1,2,64,256]{4,3,2,1,0:T(8,128)(2,1)S(1)}, u32[]{:S(2)}, u32[]{:S(2)}) collective-permute-start(bf16[4,1,2,64,256]{4,3,2,1,0:T(8,128)(2,1)S(1)} %get-tuple-element.11.even_ref.refs_1_), channel_id=1, source_target_pairs={{0,4},{2,6},{4,8},{6,10},{8,12},{10,14},{12,16},{14,18},{16,20},{1... | collective-permute-start | bytes 786440 | tf_op jit(solution)/shard_map/ppermute | solution.py:18
  6.9 9.0 %collective-permute-start.6 = (bf16[3,1,2,64,256]{4,3,2,1,0:T(8,128)(2,1)S(1)}, bf16[3,1,2,64,256]{4,3,2,1,0:T(8,128)(2,1)S(1)}, u32[]{:S(2)}, u32[]{:S(2)}) collective-permute-start(bf16[3,1,2,64,256]{4,3,2,1,0:T(8,128)(2,1)S(1)} %slice.7), channel_id=1, source_target_pairs={{0,2},{2,0},{4,6},{6,4},{8,10},{10,8},{12,14},{14,12},{16,18},{18,... | collective-permute-start | bytes 589832 | tf_op jit(solution)/shard_map/ppermute | solution.py:18
  8.4 16.9 %collective-permute-start.3 = (bf16[4,1,2,64,256]{4,3,2,1,0:T(8,128)(2,1)S(1)}, bf16[4,1,2,64,256]{4,3,2,1,0:T(8,128)(2,1)S(1)}, u32[]{:S(2)}, u32[]{:S(2)}) collective-permute-start(bf16[4,1,2,64,256]{4,3,2,1,0:T(8,128)(2,1)S(1)} %get-tuple-element.12.even_ref.refs_2_), channel_id=1, source_target_pairs={{0,4},{2,6},{4,8},{6,10},{8,12},{10,14},{12,16},{14,18},{16,20},{1... | collective-permute-start | bytes 786440 | tf_op jit(solution)/shard_map/ppermute | solution.py:18
  10.0 21.0 %collective-permute-start = (bf16[4,1,2,64,256]{4,3,2,1,0:T(8,128)(2,1)S(1)}, bf16[4,1,2,64,256]{4,3,2,1,0:T(8,128)(2,1)S(1)}, u32[]{:S(2)}, u32[]{:S(2)}) collective-permute-start(bf16[4,1,2,64,256]{4,3,2,1,0:T(8,128)(2,1)S(1)} %get-tuple-element.10.even_ref.refs_3_), channel_id=1, source_target_pairs={{0,4},{2,6},{4,8},{6,10},{8,12},{10,14},{12,16},{14,18},{16,20},{1... | collective-permute-start | bytes 786440 | tf_op jit(solution)/shard_map/ppermute | solution.py:18
  14.2 19.0 %collective-permute-start.8 = (bf16[4,1,2,64,256]{4,3,2,1,0:T(8,128)(2,1)S(1)}, bf16[4,1,2,64,256]{4,3,2,1,0:T(8,128)(2,1)S(1)}, u32[]{:S(2)}, u32[]{:S(2)}) collective-permute-start(bf16[4,1,2,64,256]{4,3,2,1,0:T(8,128)(2,1)S(1)} %shard_map.32), channel_id=1, source_target_pairs={{0,2},{2,0},{4,6},{6,4},{8,10},{10,8},{12,14},{14,12},{16,18},{18,... | collective-permute-start | bytes 786440 | tf_op jit(solution)/shard_map/ppermute | solution.py:18
  19.8 13.4 %collective-permute-start.9 = (bf16[4,1,2,64,256]{4,3,2,1,0:T(8,128)(2,1)S(1)}, bf16[4,1,2,64,256]{4,3,2,1,0:T(8,128)(2,1)S(1)}, u32[]{:S(2)}, u32[]{:S(2)}) collective-permute-start(bf16[4,1,2,64,256]{4,3,2,1,0:T(8,128)(2,1)S(1)} %shard_map.33), channel_id=1, source_target_pairs={{0,2},{2,0},{4,6},{6,4},{8,10},{10,8},{12,14},{14,12},{16,18},{18,... | collective-permute-start | bytes 786440 | tf_op jit(solution)/shard_map/ppermute | solution.py:18
  21.5 12.9 %collective-permute-start.7 = (bf16[3,1,2,64,256]{4,3,2,1,0:T(8,128)(2,1)S(1)}, bf16[3,1,2,64,256]{4,3,2,1,0:T(8,128)(2,1)S(1)}, u32[]{:S(2)}, u32[]{:S(2)}) collective-permute-start(bf16[3,1,2,64,256]{4,3,2,1,0:T(8,128)(2,1)S(1)} %collective-permute-done.6.refs_0_.odd_ref), channel_id=1, source_target_pairs={{0,4},{2,6},{4,8},{6,10},{8,12},{10,14},{12,16},{14,18},{16,20},{1... | collective-permute-start | bytes 589832 | tf_op jit(solution)/shard_map/ppermute | solution.py:18
  25.4 9.0 %collective-permute-start.5 = (bf16[4,1,2,64,256]{4,3,2,1,0:T(8,128)(2,1)S(1)}, bf16[4,1,2,64,256]{4,3,2,1,0:T(8,128)(2,1)S(1)}, u32[]{:S(2)}, u32[]{:S(2)}) collective-permute-start(bf16[4,1,2,64,256]{4,3,2,1,0:T(8,128)(2,1)S(1)} %shard_map.31), channel_id=1, source_target_pairs={{0,2},{2,0},{4,6},{6,4},{8,10},{10,8},{12,14},{14,12},{16,18},{18,... | collective-permute-start | bytes 786440 | tf_op jit(solution)/shard_map/ppermute | solution.py:18
  31.0 4.3 %collective-permute-start.4 = (bf16[1,1,2,64,256]{4,3,2,1,0:T(8,128)(2,1)S(1)}, bf16[1,1,2,64,256]{4,3,2,1,0:T(8,128)(2,1)S(1)}, u32[]{:S(2)}, u32[]{:S(2)}) collective-permute-start(bf16[1,1,2,64,256]{4,3,2,1,0:T(8,128)(2,1)S(1)} %shard_map.30), channel_id=1, source_target_pairs={{0,2},{2,0},{4,6},{6,4},{8,10},{10,8},{12,14},{14,12},{16,18},{18,... | collective-permute-start | bytes 196616 | tf_op jit(solution)/shard_map/ppermute | solution.py:18
  35.8 1.2 %collective-permute-start.10 = (f32[3,4,12]{2,1,0:T(4,128)S(1)}, f32[3,4,12]{2,1,0:T(4,128)S(1)}, u32[]{:S(2)}, u32[]{:S(2)}) collective-permute-start(f32[3,4,12]{2,1,0:T(4,128)S(1)} %shard_map.39), channel_id=1, source_target_pairs={{0,1},{1,0},{2,3},{3,2},{4,5},{5,4},{6,7},{7,6},{8,9},{9,8},{10,11... | collective-permute-start | bytes 1736 | tf_op jit(solution)/shard_map/ppermute | solution.py:18
where the time goes:
time: 37.7 us; the launch traced here: 37.5 us
  starting transfers between devices  16.1 us (43%)
  waiting for transfers between devices  14.1 us (37%)
  Pallas kernels  4.53 us (12%)
  local copies, waits for them, and re-layouts  2.22 us (6%)
  other arithmetic  0.6 us (2%)
    ppermute x11, starting transfers between devices, permuted(): lax.ppermute(block, axis, [(i, target(i) % size) for i in range(size)])  16.1 us
    ppermute x11, waiting for transfers between devices, permuted(): lax.ppermute(block, axis, [(i, target(i) % size) for i in range(size)])  14.1 us
    pallas_call x12, Pallas kernels, call(): pl.pallas_call(kernel, out_shape=out_shape, in_specs=specs, out_specs=jax...  4.53 us
    unnamed x4, local copies, waits for them, and re-layouts  1.23 us
    slice x1, local copies, waits for them, and re-layouts, local(): val[..., :depth]  0.97 us
  transfers between devices with their start and end apart: 11, of which 7 were waited for; matrix products, arithmetic and copies ran while one was open for 0% of the time, Pallas kernels for 11%

commit v1 on v0

--- a/solution.py
+++ b/solution.py
@@ -8,7 +8,7 @@
 from jax.sharding import PartitionSpec as P
 
 CUTS = 4
-GROUP = 4
+GROUP = 12
 
 VMEM = pl.BlockSpec(memory_space=pltpu.VMEM)
 

time: 37.7 us -> 37.7 us (level)
  no operation moved by 1% of the time
where the time goes in v1:
time: 37.7 us; the launch traced here: 37.6 us
  starting transfers between devices  16.1 us (43%)
  waiting for transfers between devices  14.1 us (37%)
  Pallas kernels  4.5 us (12%)
  local copies, waits for them, and re-layouts  2.22 us (6%)
  other arithmetic  0.6 us (2%)
    ppermute x11, starting transfers between devices, permuted(): lax.ppermute(block, axis, [(i, target(i) % size) for i in range(size)])  16.1 us
    ppermute x11, waiting for transfers between devices, permuted(): lax.ppermute(block, axis, [(i, target(i) % size) for i in range(size)])  14.1 us
    pallas_call x12, Pallas kernels, call(): pl.pallas_call(kernel, out_shape=out_shape, in_specs=specs, out_specs=jax...  4.5 us
    unnamed x4, local copies, waits for them, and re-layouts  1.23 us
    slice x1, local copies, waits for them, and re-layouts, local(): val[..., :depth]  0.97 us
  transfers between devices with their start and end apart: 11, of which 7 were waited for; matrix products, arithmetic and copies ran while one was open for 0% of the time, Pallas kernels for 11%

profile of v1, /device:TPU:0, one launch (start us, length us, event | category | flops | bytes accessed | tf_op | source)
XLA Modules:
  0.0 37.6 jit_solution(15505719384383281434)
XLA Ops:
  0.0 1.0 %slice.6.even_ref.refs_0_ = bf16[4,1,2,64,256]{4,3,2,1,0:T(8,128)(2,1)S(1)} slice(bf16[4,1,2,64,1024]{4,3,2,1,0:T(8,128)(2,1)} %val_ref.1), slice={[0:4], [0:1], [0:2], [0:64], [0:256]} | slice | bytes 524288 | tf_op jit(solution)/shard_map/slice | solution.py:222
  1.0 3.0 %collective-permute-start.1 = (bf16[4,1,2,64,256]{4,3,2,1,0:T(8,128)(2,1)S(1)}, bf16[4,1,2,64,256]{4,3,2,1,0:T(8,128)(2,1)S(1)}, u32[]{:S(2)}, u32[]{:S(2)}) collective-permute-start(bf16[4,1,2,64,256]{4,3,2,1,0:T(8,128)(2,1)S(1)} %slice.6.even_ref.refs_0_), channel_id=1, source_target_pairs={{0,4},{2,6},{4,8},{6,10},{8,12},{10,14},{12,16},{14,18},{16,20},{1... | collective-permute-start | bytes 786440 | tf_op jit(solution)/shard_map/ppermute | solution.py:18
  4.0 0.0 copy-start.1
  4.0 1.2 %copy-done.1 = bf16[4,1,2,64,1024]{4,3,2,1,0:T(8,128)(2,1)S(1)} copy-done((bf16[4,1,2,64,1024]{4,3,2,1,0:T(8,128)(2,1)S(1)}, bf16[4,1,2,64,1024]{4,3,2,1,0:T(8,128)(2,1)}, u32[]{:S(2)}) %copy-start.1) | copy-done | bytes 1048600
  5.2 0.0 copy-start
  5.2 0.1 shard_map.28
  5.3 1.6 %collective-permute-start.2 = (bf16[4,1,2,64,256]{4,3,2,1,0:T(8,128)(2,1)S(1)}, bf16[4,1,2,64,256]{4,3,2,1,0:T(8,128)(2,1)S(1)}, u32[]{:S(2)}, u32[]{:S(2)}) collective-permute-start(bf16[4,1,2,64,256]{4,3,2,1,0:T(8,128)(2,1)S(1)} %get-tuple-element.11.even_ref.refs_1_), channel_id=1, source_target_pairs={{0,4},{2,6},{4,8},{6,10},{8,12},{10,14},{12,16},{14,18},{16,20},{1... | collective-permute-start | bytes 786440 | tf_op jit(solution)/shard_map/ppermute | solution.py:18
  6.9 1.6 %collective-permute-start.6 = (bf16[3,1,2,64,256]{4,3,2,1,0:T(8,128)(2,1)S(1)}, bf16[3,1,2,64,256]{4,3,2,1,0:T(8,128)(2,1)S(1)}, u32[]{:S(2)}, u32[]{:S(2)}) collective-permute-start(bf16[3,1,2,64,256]{4,3,2,1,0:T(8,128)(2,1)S(1)} %slice.7), channel_id=1, source_target_pairs={{0,2},{2,0},{4,6},{6,4},{8,10},{10,8},{12,14},{14,12},{16,18},{18,... | collective-permute-start | bytes 589832 | tf_op jit(solution)/shard_map/ppermute | solution.py:18
  8.4 1.5 %collective-permute-start.3 = (bf16[4,1,2,64,256]{4,3,2,1,0:T(8,128)(2,1)S(1)}, bf16[4,1,2,64,256]{4,3,2,1,0:T(8,128)(2,1)S(1)}, u32[]{:S(2)}, u32[]{:S(2)}) collective-permute-start(bf16[4,1,2,64,256]{4,3,2,1,0:T(8,128)(2,1)S(1)} %get-tuple-element.12.even_ref.refs_2_), channel_id=1, source_target_pairs={{0,4},{2,6},{4,8},{6,10},{8,12},{10,14},{12,16},{14,18},{16,20},{1... | collective-permute-start | bytes 786440 | tf_op jit(solution)/shard_map/ppermute | solution.py:18
  10.0 1.5 %collective-permute-start = (bf16[4,1,2,64,256]{4,3,2,1,0:T(8,128)(2,1)S(1)}, bf16[4,1,2,64,256]{4,3,2,1,0:T(8,128)(2,1)S(1)}, u32[]{:S(2)}, u32[]{:S(2)}) collective-permute-start(bf16[4,1,2,64,256]{4,3,2,1,0:T(8,128)(2,1)S(1)} %get-tuple-element.10.even_ref.refs_3_), channel_id=1, source_target_pairs={{0,4},{2,6},{4,8},{6,10},{8,12},{10,14},{12,16},{14,18},{16,20},{1... | collective-permute-start | bytes 786440 | tf_op jit(solution)/shard_map/ppermute | solution.py:18
  11.5 2.7 %collective-permute-done.1.refs_0_.odd_ref = bf16[4,1,2,64,256]{4,3,2,1,0:T(8,128)(2,1)S(1)} collective-permute-done((bf16[4,1,2,64,256]{4,3,2,1,0:T(8,128)(2,1)S(1)}, bf16[4,1,2,64,256]{4,3,2,1,0:T(8,128)(2,1)S(1)}, u32[]{:S(2)}, u32[]{:S(2)}) %collective-permute-start.1) | collective-permute-done | bytes 262176 | tf_op jit(solution)/shard_map/ppermute | solution.py:18
  14.2 1.7 %collective-permute-start.8 = (bf16[4,1,2,64,256]{4,3,2,1,0:T(8,128)(2,1)S(1)}, bf16[4,1,2,64,256]{4,3,2,1,0:T(8,128)(2,1)S(1)}, u32[]{:S(2)}, u32[]{:S(2)}) collective-permute-start(bf16[4,1,2,64,256]{4,3,2,1,0:T(8,128)(2,1)S(1)} %shard_map.32), channel_id=1, source_target_pairs={{0,2},{2,0},{4,6},{6,4},{8,10},{10,8},{12,14},{14,12},{16,18},{18,... | collective-permute-start | bytes 786440 | tf_op jit(solution)/shard_map/ppermute | solution.py:18
  15.9 0.0 collective-permute-done.6.refs_0_.odd_ref
  15.9 3.9 %collective-permute-done.2.refs_1_.odd_ref = bf16[4,1,2,64,256]{4,3,2,1,0:T(8,128)(2,1)S(1)} collective-permute-done((bf16[4,1,2,64,256]{4,3,2,1,0:T(8,128)(2,1)S(1)}, bf16[4,1,2,64,256]{4,3,2,1,0:T(8,128)(2,1)S(1)}, u32[]{:S(2)}, u32[]{:S(2)}) %collective-permute-start.2) | collective-permute-done | bytes 262176 | tf_op jit(solution)/shard_map/ppermute | solution.py:18
  19.8 1.7 %collective-permute-start.9 = (bf16[4,1,2,64,256]{4,3,2,1,0:T(8,128)(2,1)S(1)}, bf16[4,1,2,64,256]{4,3,2,1,0:T(8,128)(2,1)S(1)}, u32[]{:S(2)}, u32[]{:S(2)}) collective-permute-start(bf16[4,1,2,64,256]{4,3,2,1,0:T(8,128)(2,1)S(1)} %shard_map.33), channel_id=1, source_target_pairs={{0,2},{2,0},{4,6},{6,4},{8,10},{10,8},{12,14},{14,12},{16,18},{18,... | collective-permute-start | bytes 786440 | tf_op jit(solution)/shard_map/ppermute | solution.py:18
  21.5 0.0 collective-permute-start.7
  21.5 3.9 %collective-permute-done.3.refs_2_.odd_ref = bf16[4,1,2,64,256]{4,3,2,1,0:T(8,128)(2,1)S(1)} collective-permute-done((bf16[4,1,2,64,256]{4,3,2,1,0:T(8,128)(2,1)S(1)}, bf16[4,1,2,64,256]{4,3,2,1,0:T(8,128)(2,1)S(1)}, u32[]{:S(2)}, u32[]{:S(2)}) %collective-permute-start.3) | collective-permute-done | bytes 262176 | tf_op jit(solution)/shard_map/ppermute | solution.py:18
  25.4 1.7 %collective-permute-start.5 = (bf16[4,1,2,64,256]{4,3,2,1,0:T(8,128)(2,1)S(1)}, bf16[4,1,2,64,256]{4,3,2,1,0:T(8,128)(2,1)S(1)}, u32[]{:S(2)}, u32[]{:S(2)}) collective-permute-start(bf16[4,1,2,64,256]{4,3,2,1,0:T(8,128)(2,1)S(1)} %shard_map.31), channel_id=1, source_target_pairs={{0,2},{2,0},{4,6},{6,4},{8,10},{10,8},{12,14},{14,12},{16,18},{18,... | collective-permute-start | bytes 786440 | tf_op jit(solution)/shard_map/ppermute | solution.py:18
  27.2 0.0 copy-done
  27.2 1.1 %shard_map.37.own_ref = f32[4,12]{1,0:T(4,128)S(1)} custom-call(bf16[12,1,2,64,1024]{4,3,2,1,0:T(8,128)(2,1)S(1)} %copy-done, bf16[4,1,2,64,256]{4,3,2,1,0:T(8,128)(2,1)S(1)} %slice.6.even_ref.refs_0_, bf16[4,1,2,64,256]{4,3,2,1,0:T(8,128)(2,1)S(1)} %get-tuple-element.11.even_ref.refs_1_, bf16[4,1,2,64,256]{4,3,2,1,0:T(8,128)(2,1)S(1)} %get-tuple-element.12.even_ref.refs_2_, ...), custom_call_target="tpu_custom_call" | custom-call | flops 805306368 | bytes 4194496 | tf_op jit(solution)/shard_map/pallas_call | solution.py:23
  28.3 0.8 %shard_map.29.refs_0_.grams_ref = f32[1,2,768,256]{3,2,1,0:T(8,128)S(1)} custom-call(bf16[12,1,2,64,1024]{4,3,2,1,0:T(8,128)(2,1)S(1)} %copy-done, bf16[4,1,2,64,256]{4,3,2,1,0:T(8,128)(2,1)S(1)} %collective-permute-done.1.refs_0_.odd_ref, bf16[4,1,2,64,256]{4,3,2,1,0:T(8,128)(2,1)S(1)} %collective-permute-done.2.refs_1_.odd_ref, ...), custom_call_target="tpu_custom_call" | custom-call | flops 805306368 | bytes 5505024 | tf_op jit(solution)/shard_map/pallas_call | solution.py:23
  29.1 1.9 %collective-permute-done.odd_ref.part_ref = bf16[4,1,2,64,256]{4,3,2,1,0:T(8,128)(2,1)S(1)} collective-permute-done((bf16[4,1,2,64,256]{4,3,2,1,0:T(8,128)(2,1)S(1)}, bf16[4,1,2,64,256]{4,3,2,1,0:T(8,128)(2,1)S(1)}, u32[]{:S(2)}, u32[]{:S(2)}) %collective-permute-start) | collective-permute-done | bytes 262176 | tf_op jit(solution)/shard_map/ppermute | solution.py:18
  31.0 1.7 %collective-permute-start.4 = (bf16[1,1,2,64,256]{4,3,2,1,0:T(8,128)(2,1)S(1)}, bf16[1,1,2,64,256]{4,3,2,1,0:T(8,128)(2,1)S(1)}, u32[]{:S(2)}, u32[]{:S(2)}) collective-permute-start(bf16[1,1,2,64,256]{4,3,2,1,0:T(8,128)(2,1)S(1)} %shard_map.30), channel_id=1, source_target_pairs={{0,2},{2,0},{4,6},{6,4},{8,10},{10,8},{12,14},{14,12},{16,18},{18,... | collective-permute-start | bytes 196616 | tf_op jit(solution)/shard_map/ppermute | solution.py:18
  32.7 0.5 %shard_map.38.second_ref = f32[4,12]{1,0:T(4,128)S(1)} custom-call(bf16[12,1,2,64,1024]{4,3,2,1,0:T(8,128)(2,1)S(1)} %copy-done, bf16[4,1,2,64,256]{4,3,2,1,0:T(8,128)(2,1)S(1)} %collective-permute-done.odd_ref.part_ref, f32[1,2,768,256]{3,2,1,0:T(8,128)S(1)} %shard_map.29.refs_0_.grams_ref), custom_call_target="tpu_custom_call" | custom-call | flops 201326592 | bytes 4980928 | tf_op jit(solution)/shard_map/pallas_call | solution.py:23
  33.2 0.0 collective-permute-done.8.refs_0_
  33.2 0.0 collective-permute-done.9.refs_1_
  33.3 0.6 %shard_map.34.refs_0_.grams_ref = f32[1,2,768,256]{3,2,1,0:T(8,128)S(1)} custom-call(bf16[12,1,2,64,1024]{4,3,2,1,0:T(8,128)(2,1)S(1)} %copy-done, bf16[4,1,2,64,256]{4,3,2,1,0:T(8,128)(2,1)S(1)} %collective-permute-done.8.refs_0_, bf16[4,1,2,64,256]{4,3,2,1,0:T(8,128)(2,1)S(1)} %collective-permute-done.9.refs_1_), custom_call_target="tpu_custom_call" | custom-call | flops 402653184 | bytes 5242880 | tf_op jit(solution)/shard_map/pallas_call | solution.py:23
  33.9 0.5 %collective-permute-done.7.even_ref = bf16[3,1,2,64,256]{4,3,2,1,0:T(8,128)(2,1)S(1)} collective-permute-done((bf16[3,1,2,64,256]{4,3,2,1,0:T(8,128)(2,1)S(1)}, bf16[3,1,2,64,256]{4,3,2,1,0:T(8,128)(2,1)S(1)}, u32[]{:S(2)}, u32[]{:S(2)}) %collective-permute-start.7) | collective-permute-done | bytes 196640 | tf_op jit(solution)/shard_map/ppermute | solution.py:18
  34.4 0.0 collective-permute-done.5.part_ref
  34.4 0.8 %shard_map.36 = (f32[1,2,768,64]{3,2,1,0:T(8,128)S(1)}, f32[3,12]{1,0:T(4,128)S(1)}) custom-call(bf16[12,1,2,64,1024]{4,3,2,1,0:T(8,128)(2,1)S(1)} %copy-done, bf16[4,1,2,64,256]{4,3,2,1,0:T(8,128)(2,1)S(1)} %collective-permute-done.5.part_ref, bf16[3,1,2,64,256]{4,3,2,1,0:T(8,128)(2,1)S(1)} %shard_map.35.last_ref, ...), custom_call_target="tpu_custom_call" | custom-call | flops 201326592 | bytes 5570704 | tf_op jit(solution)/shard_map/pallas_call | solution.py:23
  35.2 0.1 collective-permute-done.4.end_ref
  35.3 0.5 %shard_map.39 = f32[3,4,12]{2,1,0:T(4,128)S(1)} custom-call(bf16[12,1,2,64,1024]{4,3,2,1,0:T(8,128)(2,1)S(1)} %copy-done, bf16[1,1,2,64,256]{4,3,2,1,0:T(8,128)(2,1)S(1)} %collective-permute-done.4.end_ref, f32[1,2,768,64]{3,2,1,0:T(8,128)S(1)} %get-tuple-element.13.ends_ref, f32[4,12]{1,0:T(4,128)S(1)} %shard_map.37.own_ref, ...), custom_call_target="tpu_custom_call" | custom-call | flops 50331648 | bytes 3605584 | tf_op jit(solution)/shard_map/pallas_call | solution.py:23
  35.8 0.0 collective-permute-start.10
  35.8 1.2 %collective-permute-done.10 = f32[3,4,12]{2,1,0:T(4,128)S(1)} collective-permute-done((f32[3,4,12]{2,1,0:T(4,128)S(1)}, f32[3,4,12]{2,1,0:T(4,128)S(1)}, u32[]{:S(2)}, u32[]{:S(2)}) %collective-permute-start.10) | collective-permute-done | bytes 608 | tf_op jit(solution)/shard_map/ppermute | solution.py:18
  37.0 0.6 %add_bitcast_fusion = f32[12,3,4]{0,2,1:T(4,128)} fusion(f32[3,4,12]{2,1,0:T(4,128)S(1)} %shard_map.39, f32[3,4,12]{2,1,0:T(4,128)S(1)} %collective-permute-done.10), kind=kLoop, calls=%fused_computation | loop fusion | flops 144 | bytes 1728 | tf_op jit(solution)/shard_map/transpose | solution.py:247
  (6 shorter events, 0.1 us)
Async XLA Ops:
  1.0 13.2 %collective-permute-start.1 = (bf16[4,1,2,64,256]{4,3,2,1,0:T(8,128)(2,1)S(1)}, bf16[4,1,2,64,256]{4,3,2,1,0:T(8,128)(2,1)S(1)}, u32[]{:S(2)}, u32[]{:S(2)}) collective-permute-start(bf16[4,1,2,64,256]{4,3,2,1,0:T(8,128)(2,1)S(1)} %slice.6.even_ref.refs_0_), channel_id=1, source_target_pairs={{0,4},{2,6},{4,8},{6,10},{8,12},{10,14},{12,16},{14,18},{16,20},{1... | collective-permute-start | bytes 786440 | tf_op jit(solution)/shard_map/ppermute | solution.py:18
  4.0 1.2 %copy-start.1 = (bf16[4,1,2,64,1024]{4,3,2,1,0:T(8,128)(2,1)S(1)}, bf16[4,1,2,64,1024]{4,3,2,1,0:T(8,128)(2,1)}, u32[]{:S(2)}) copy-start(bf16[4,1,2,64,1024]{4,3,2,1,0:T(8,128)(2,1)} %val_ref.1) | copy-start | bytes 3145732
  5.2 21.9 %copy-start = (bf16[12,1,2,64,1024]{4,3,2,1,0:T(8,128)(2,1)S(1)}, bf16[12,1,2,64,1024]{4,3,2,1,0:T(8,128)(2,1)}, u32[]{:S(2)}) copy-start(bf16[12,1,2,64,1024]{4,3,2,1,0:T(8,128)(2,1)} %train_ref.11) | copy-start | bytes 9437188
  5.3 14.5 %collective-permute-start.2 = (bf16[4,1,2,64,256]{4,3,2,1,0:T(8,128)(2,1)S(1)}, bf16[4,1,2,64,256]{4,3,2,1,0:T(8,128)(2,1)S(1)}, u32[]{:S(2)}, u32[]{:S(2)}) collective-permute-start(bf16[4,1,2,64,256]{4,3,2,1,0:T(8,128)(2,1)S(1)} %get-tuple-element.11.even_ref.refs_1_), channel_id=1, source_target_pairs={{0,4},{2,6},{4,8},{6,10},{8,12},{10,14},{12,16},{14,18},{16,20},{1... | collective-permute-start | bytes 786440 | tf_op jit(solution)/shard_map/ppermute | solution.py:18
  6.9 9.0 %collective-permute-start.6 = (bf16[3,1,2,64,256]{4,3,2,1,0:T(8,128)(2,1)S(1)}, bf16[3,1,2,64,256]{4,3,2,1,0:T(8,128)(2,1)S(1)}, u32[]{:S(2)}, u32[]{:S(2)}) collective-permute-start(bf16[3,1,2,64,256]{4,3,2,1,0:T(8,128)(2,1)S(1)} %slice.7), channel_id=1, source_target_pairs={{0,2},{2,0},{4,6},{6,4},{8,10},{10,8},{12,14},{14,12},{16,18},{18,... | collective-permute-start | bytes 589832 | tf_op jit(solution)/shard_map/ppermute | solution.py:18
  8.4 16.9 %collective-permute-start.3 = (bf16[4,1,2,64,256]{4,3,2,1,0:T(8,128)(2,1)S(1)}, bf16[4,1,2,64,256]{4,3,2,1,0:T(8,128)(2,1)S(1)}, u32[]{:S(2)}, u32[]{:S(2)}) collective-permute-start(bf16[4,1,2,64,256]{4,3,2,1,0:T(8,128)(2,1)S(1)} %get-tuple-element.12.even_ref.refs_2_), channel_id=1, source_target_pairs={{0,4},{2,6},{4,8},{6,10},{8,12},{10,14},{12,16},{14,18},{16,20},{1... | collective-permute-start | bytes 786440 | tf_op jit(solution)/shard_map/ppermute | solution.py:18
  10.0 21.0 %collective-permute-start = (bf16[4,1,2,64,256]{4,3,2,1,0:T(8,128)(2,1)S(1)}, bf16[4,1,2,64,256]{4,3,2,1,0:T(8,128)(2,1)S(1)}, u32[]{:S(2)}, u32[]{:S(2)}) collective-permute-start(bf16[4,1,2,64,256]{4,3,2,1,0:T(8,128)(2,1)S(1)} %get-tuple-element.10.even_ref.refs_3_), channel_id=1, source_target_pairs={{0,4},{2,6},{4,8},{6,10},{8,12},{10,14},{12,16},{14,18},{16,20},{1... | collective-permute-start | bytes 786440 | tf_op jit(solution)/shard_map/ppermute | solution.py:18
  14.2 19.0 %collective-permute-start.8 = (bf16[4,1,2,64,256]{4,3,2,1,0:T(8,128)(2,1)S(1)}, bf16[4,1,2,64,256]{4,3,2,1,0:T(8,128)(2,1)S(1)}, u32[]{:S(2)}, u32[]{:S(2)}) collective-permute-start(bf16[4,1,2,64,256]{4,3,2,1,0:T(8,128)(2,1)S(1)} %shard_map.32), channel_id=1, source_target_pairs={{0,2},{2,0},{4,6},{6,4},{8,10},{10,8},{12,14},{14,12},{16,18},{18,... | collective-permute-start | bytes 786440 | tf_op jit(solution)/shard_map/ppermute | solution.py:18
  19.8 13.4 %collective-permute-start.9 = (bf16[4,1,2,64,256]{4,3,2,1,0:T(8,128)(2,1)S(1)}, bf16[4,1,2,64,256]{4,3,2,1,0:T(8,128)(2,1)S(1)}, u32[]{:S(2)}, u32[]{:S(2)}) collective-permute-start(bf16[4,1,2,64,256]{4,3,2,1,0:T(8,128)(2,1)S(1)} %shard_map.33), channel_id=1, source_target_pairs={{0,2},{2,0},{4,6},{6,4},{8,10},{10,8},{12,14},{14,12},{16,18},{18,... | collective-permute-start | bytes 786440 | tf_op jit(solution)/shard_map/ppermute | solution.py:18
  21.5 12.9 %collective-permute-start.7 = (bf16[3,1,2,64,256]{4,3,2,1,0:T(8,128)(2,1)S(1)}, bf16[3,1,2,64,256]{4,3,2,1,0:T(8,128)(2,1)S(1)}, u32[]{:S(2)}, u32[]{:S(2)}) collective-permute-start(bf16[3,1,2,64,256]{4,3,2,1,0:T(8,128)(2,1)S(1)} %collective-permute-done.6.refs_0_.odd_ref), channel_id=1, source_target_pairs={{0,4},{2,6},{4,8},{6,10},{8,12},{10,14},{12,16},{14,18},{16,20},{1... | collective-permute-start | bytes 589832 | tf_op jit(solution)/shard_map/ppermute | solution.py:18
  25.4 9.0 %collective-permute-start.5 = (bf16[4,1,2,64,256]{4,3,2,1,0:T(8,128)(2,1)S(1)}, bf16[4,1,2,64,256]{4,3,2,1,0:T(8,128)(2,1)S(1)}, u32[]{:S(2)}, u32[]{:S(2)}) collective-permute-start(bf16[4,1,2,64,256]{4,3,2,1,0:T(8,128)(2,1)S(1)} %shard_map.31), channel_id=1, source_target_pairs={{0,2},{2,0},{4,6},{6,4},{8,10},{10,8},{12,14},{14,12},{16,18},{18,... | collective-permute-start | bytes 786440 | tf_op jit(solution)/shard_map/ppermute | solution.py:18
  31.0 4.3 %collective-permute-start.4 = (bf16[1,1,2,64,256]{4,3,2,1,0:T(8,128)(2,1)S(1)}, bf16[1,1,2,64,256]{4,3,2,1,0:T(8,128)(2,1)S(1)}, u32[]{:S(2)}, u32[]{:S(2)}) collective-permute-start(bf16[1,1,2,64,256]{4,3,2,1,0:T(8,128)(2,1)S(1)} %shard_map.30), channel_id=1, source_target_pairs={{0,2},{2,0},{4,6},{6,4},{8,10},{10,8},{12,14},{14,12},{16,18},{18,... | collective-permute-start | bytes 196616 | tf_op jit(solution)/shard_map/ppermute | solution.py:18
  35.8 1.2 %collective-permute-start.10 = (f32[3,4,12]{2,1,0:T(4,128)S(1)}, f32[3,4,12]{2,1,0:T(4,128)S(1)}, u32[]{:S(2)}, u32[]{:S(2)}) collective-permute-start(f32[3,4,12]{2,1,0:T(4,128)S(1)} %shard_map.39), channel_id=1, source_target_pairs={{0,1},{1,0},{2,3},{3,2},{4,5},{5,4},{6,7},{7,6},{8,9},{9,8},{10,11... | collective-permute-start | bytes 1736 | tf_op jit(solution)/shard_map/ppermute | solution.py:18

commit v2 on v0

--- a/solution.py
+++ b/solution.py
@@ -11,6 +11,7 @@
 GROUP = 4
 
 VMEM = pl.BlockSpec(memory_space=pltpu.VMEM)
+HBM = pl.BlockSpec(memory_space=pltpu.HBM)
 
 
 def permuted(block, axis, target):
@@ -92,6 +93,17 @@
         ref[...] = val_ref[..., c * depth : (c + 1) * depth]
 
 
+def first_cut_kernel(val_ref, part_ref, sems):
+    copies = [
+        pltpu.make_async_copy(val_ref.at[v, ..., : part_ref.shape[-1]], part_ref.at[v], sems.at[v])
+        for v in range(part_ref.shape[0])
+    ]
+    for copy in copies:
+        copy.start()
+    for copy in copies:
+        copy.wait()
+
+
 def scores_kernel(train_ref, *refs):
     *val_refs, out_ref = refs
     out_ref[...] = scores(train_ref, val_refs)
@@ -201,10 +213,15 @@
     out_ref[2] = second_ref[...]
 
 
+def sum_kernel(a_ref, b_ref, out_ref):
+    out_ref[...] = a_ref[...] + b_ref[...]
+
+
 def summed(rows, axis):
     if lax.axis_size(axis) != 2:
         return lax.psum(rows, axis)
-    return rows + permuted(rows, axis, lambda i: i ^ 1)
+    shape = jax.ShapeDtypeStruct(rows.shape, rows.dtype)
+    return call(sum_kernel, shape, [VMEM] * 2, [rows, permuted(rows, axis, lambda i: i ^ 1)])
 
 
 def local(train, val):
@@ -219,7 +236,9 @@
     grams = jax.ShapeDtypeStruct((layers, 2, examples * tokens, count * tokens), jnp.float32)
 
     detour = val[: count - 1, ..., (cuts - 1) * depth :]
-    parts = [val[..., :depth], *call(cut_kernel, [part] * (cuts - 1), [VMEM], [val])]
+    sems = [pltpu.SemaphoreType.DMA((count,))]
+    first_part = call(first_cut_kernel, part, [HBM], [val], scratch=sems, vmem=107 << 19)
+    parts = [first_part, *call(cut_kernel, [part] * (cuts - 1), [VMEM], [val])]
     second = [permuted(x, "blk", lambda i: i + 2) for x in parts]
     near_last = permuted(detour, "blk", lambda i: i ^ 1)
     far_last = permuted(near_last, "blk", lambda i: i + 2)

time: 37.7 us -> 37.8 us (level)
  local copies, waits for them, and re-layouts: 2.22 us -> 0.03 us
  Pallas kernels: 4.53 us -> 6.18 us
  waiting for transfers between devices: 14.1 us -> 15.3 us
  other arithmetic: 0.6 us -> 0 us
    pallas_call x12 -> x14, Pallas kernels: 4.53 us -> 6.18 us  [call(): pl.pallas_call(kernel, out_shape=out_shape, in_specs=specs, out_specs=jax...]
    ppermute x11, waiting for transfers between devices: 14.1 us -> 15.3 us  [permuted(): lax.ppermute(block, axis, [(i, target(i) % size) for i in range(size)])]
    unnamed x4, local copies, waits for them, and re-layouts: 1.23 us -> 0.01 us
    slice x1 -> x0, local copies, waits for them, and re-layouts: 0.97 us -> none  [local(): val[..., :depth]]
    transpose x1 -> x0, other arithmetic: 0.6 us -> none  [local(): return summed(partial_rows, 'layer').transpose(2, 0, 1)]
where the time goes in v2:
time: 37.8 us; the launch traced here: 37.6 us
  starting transfers between devices  16.1 us (43%)
  waiting for transfers between devices  15.3 us (40%)
  Pallas kernels  6.18 us (16%)
    ppermute x11, starting transfers between devices, permuted(): lax.ppermute(block, axis, [(i, target(i) % size) for i in range(size)])  16.1 us
    ppermute x11, waiting for transfers between devices, permuted(): lax.ppermute(block, axis, [(i, target(i) % size) for i in range(size)])  15.3 us
    pallas_call x14, Pallas kernels, call(): pl.pallas_call(kernel, out_shape=out_shape, in_specs=specs, out_specs=jax...  6.18 us
  transfers between devices with their start and end apart: 11, of which 7 were waited for; matrix products, arithmetic and copies ran while one was open for 0% of the time, Pallas kernels for 11%

profile of v2, /device:TPU:0, one launch (start us, length us, event | category | flops | bytes accessed | tf_op | source)
XLA Modules:
  0.0 37.6 jit_solution(14424937393293904025)
XLA Ops:
  0.0 0.0 copy-start.1
  0.0 1.1 %shard_map.29.even_ref.refs_0_ = bf16[4,1,2,64,256]{4,3,2,1,0:T(8,128)(2,1)S(1)} custom-call(bf16[4,1,2,64,1024]{4,3,2,1,0:T(8,128)(2,1)} %val_ref.3), custom_call_target="tpu_custom_call" | custom-call | bytes 1310720 | tf_op jit(solution)/shard_map/pallas_call | solution.py:24
  1.1 3.0 %collective-permute-start.1 = (bf16[4,1,2,64,256]{4,3,2,1,0:T(8,128)(2,1)S(1)}, bf16[4,1,2,64,256]{4,3,2,1,0:T(8,128)(2,1)S(1)}, u32[]{:S(2)}, u32[]{:S(2)}) collective-permute-start(bf16[4,1,2,64,256]{4,3,2,1,0:T(8,128)(2,1)S(1)} %shard_map.29.even_ref.refs_0_), channel_id=1, source_target_pairs={{0,4},{2,6},{4,8},{6,10},{8,12},{10,14},{12,16},{14,18},{16,20},{1... | collective-permute-start | bytes 786440 | tf_op jit(solution)/shard_map/ppermute | solution.py:19
  4.1 0.0 copy-done.1
  4.1 0.0 copy-start
  4.1 0.1 shard_map.28
  4.2 1.6 %collective-permute-start.2 = (bf16[4,1,2,64,256]{4,3,2,1,0:T(8,128)(2,1)S(1)}, bf16[4,1,2,64,256]{4,3,2,1,0:T(8,128)(2,1)S(1)}, u32[]{:S(2)}, u32[]{:S(2)}) collective-permute-start(bf16[4,1,2,64,256]{4,3,2,1,0:T(8,128)(2,1)S(1)} %get-tuple-element.11.even_ref.refs_1_), channel_id=1, source_target_pairs={{0,4},{2,6},{4,8},{6,10},{8,12},{10,14},{12,16},{14,18},{16,20},{1... | collective-permute-start | bytes 786440 | tf_op jit(solution)/shard_map/ppermute | solution.py:19
  5.8 1.6 %collective-permute-start.6 = (bf16[3,1,2,64,256]{4,3,2,1,0:T(8,128)(2,1)S(1)}, bf16[3,1,2,64,256]{4,3,2,1,0:T(8,128)(2,1)S(1)}, u32[]{:S(2)}, u32[]{:S(2)}) collective-permute-start(bf16[3,1,2,64,256]{4,3,2,1,0:T(8,128)(2,1)S(1)} %slice.3), channel_id=1, source_target_pairs={{0,2},{2,0},{4,6},{6,4},{8,10},{10,8},{12,14},{14,12},{16,18},{18,... | collective-permute-start | bytes 589832 | tf_op jit(solution)/shard_map/ppermute | solution.py:19
  7.3 1.5 %collective-permute-start.3 = (bf16[4,1,2,64,256]{4,3,2,1,0:T(8,128)(2,1)S(1)}, bf16[4,1,2,64,256]{4,3,2,1,0:T(8,128)(2,1)S(1)}, u32[]{:S(2)}, u32[]{:S(2)}) collective-permute-start(bf16[4,1,2,64,256]{4,3,2,1,0:T(8,128)(2,1)S(1)} %get-tuple-element.12.even_ref.refs_2_), channel_id=1, source_target_pairs={{0,4},{2,6},{4,8},{6,10},{8,12},{10,14},{12,16},{14,18},{16,20},{1... | collective-permute-start | bytes 786440 | tf_op jit(solution)/shard_map/ppermute | solution.py:19
  8.8 1.5 %collective-permute-start = (bf16[4,1,2,64,256]{4,3,2,1,0:T(8,128)(2,1)S(1)}, bf16[4,1,2,64,256]{4,3,2,1,0:T(8,128)(2,1)S(1)}, u32[]{:S(2)}, u32[]{:S(2)}) collective-permute-start(bf16[4,1,2,64,256]{4,3,2,1,0:T(8,128)(2,1)S(1)} %get-tuple-element.10.even_ref.refs_3_), channel_id=1, source_target_pairs={{0,4},{2,6},{4,8},{6,10},{8,12},{10,14},{12,16},{14,18},{16,20},{1... | collective-permute-start | bytes 786440 | tf_op jit(solution)/shard_map/ppermute | solution.py:19
  10.4 3.9 %collective-permute-done.1.refs_0_.odd_ref = bf16[4,1,2,64,256]{4,3,2,1,0:T(8,128)(2,1)S(1)} collective-permute-done((bf16[4,1,2,64,256]{4,3,2,1,0:T(8,128)(2,1)S(1)}, bf16[4,1,2,64,256]{4,3,2,1,0:T(8,128)(2,1)S(1)}, u32[]{:S(2)}, u32[]{:S(2)}) %collective-permute-start.1) | collective-permute-done | bytes 262176 | tf_op jit(solution)/shard_map/ppermute | solution.py:19
  14.3 1.7 %collective-permute-start.8 = (bf16[4,1,2,64,256]{4,3,2,1,0:T(8,128)(2,1)S(1)}, bf16[4,1,2,64,256]{4,3,2,1,0:T(8,128)(2,1)S(1)}, u32[]{:S(2)}, u32[]{:S(2)}) collective-permute-start(bf16[4,1,2,64,256]{4,3,2,1,0:T(8,128)(2,1)S(1)} %shard_map.33), channel_id=1, source_target_pairs={{0,2},{2,0},{4,6},{6,4},{8,10},{10,8},{12,14},{14,12},{16,18},{18,... | collective-permute-start | bytes 786440 | tf_op jit(solution)/shard_map/ppermute | solution.py:19
  16.0 0.0 collective-permute-done.6.refs_0_.odd_ref
  16.0 3.9 %collective-permute-done.2.refs_1_.odd_ref = bf16[4,1,2,64,256]{4,3,2,1,0:T(8,128)(2,1)S(1)} collective-permute-done((bf16[4,1,2,64,256]{4,3,2,1,0:T(8,128)(2,1)S(1)}, bf16[4,1,2,64,256]{4,3,2,1,0:T(8,128)(2,1)S(1)}, u32[]{:S(2)}, u32[]{:S(2)}) %collective-permute-start.2) | collective-permute-done | bytes 262176 | tf_op jit(solution)/shard_map/ppermute | solution.py:19
  19.9 1.7 %collective-permute-start.9 = (bf16[4,1,2,64,256]{4,3,2,1,0:T(8,128)(2,1)S(1)}, bf16[4,1,2,64,256]{4,3,2,1,0:T(8,128)(2,1)S(1)}, u32[]{:S(2)}, u32[]{:S(2)}) collective-permute-start(bf16[4,1,2,64,256]{4,3,2,1,0:T(8,128)(2,1)S(1)} %shard_map.34), channel_id=1, source_target_pairs={{0,2},{2,0},{4,6},{6,4},{8,10},{10,8},{12,14},{14,12},{16,18},{18,... | collective-permute-start | bytes 786440 | tf_op jit(solution)/shard_map/ppermute | solution.py:19
  21.6 0.0 collective-permute-start.7
  21.6 3.9 %collective-permute-done.3.refs_2_.odd_ref = bf16[4,1,2,64,256]{4,3,2,1,0:T(8,128)(2,1)S(1)} collective-permute-done((bf16[4,1,2,64,256]{4,3,2,1,0:T(8,128)(2,1)S(1)}, bf16[4,1,2,64,256]{4,3,2,1,0:T(8,128)(2,1)S(1)}, u32[]{:S(2)}, u32[]{:S(2)}) %collective-permute-start.3) | collective-permute-done | bytes 262176 | tf_op jit(solution)/shard_map/ppermute | solution.py:19
  25.5 1.7 %collective-permute-start.5 = (bf16[4,1,2,64,256]{4,3,2,1,0:T(8,128)(2,1)S(1)}, bf16[4,1,2,64,256]{4,3,2,1,0:T(8,128)(2,1)S(1)}, u32[]{:S(2)}, u32[]{:S(2)}) collective-permute-start(bf16[4,1,2,64,256]{4,3,2,1,0:T(8,128)(2,1)S(1)} %shard_map.32), channel_id=1, source_target_pairs={{0,2},{2,0},{4,6},{6,4},{8,10},{10,8},{12,14},{14,12},{16,18},{18,... | collective-permute-start | bytes 786440 | tf_op jit(solution)/shard_map/ppermute | solution.py:19
  27.3 0.0 copy-done
  27.3 1.2 %shard_map.38.own_ref = f32[4,12]{1,0:T(4,128)S(1)} custom-call(bf16[12,1,2,64,1024]{4,3,2,1,0:T(8,128)(2,1)S(1)} %copy-done, bf16[4,1,2,64,256]{4,3,2,1,0:T(8,128)(2,1)S(1)} %shard_map.29.even_ref.refs_0_, bf16[4,1,2,64,256]{4,3,2,1,0:T(8,128)(2,1)S(1)} %get-tuple-element.11.even_ref.refs_1_, ...), custom_call_target="tpu_custom_call" | custom-call | flops 805306368 | bytes 4194496 | tf_op jit(solution)/shard_map/pallas_call | solution.py:24
  28.4 0.8 %shard_map.30.refs_0_.grams_ref = f32[1,2,768,256]{3,2,1,0:T(8,128)S(1)} custom-call(bf16[12,1,2,64,1024]{4,3,2,1,0:T(8,128)(2,1)S(1)} %copy-done, bf16[4,1,2,64,256]{4,3,2,1,0:T(8,128)(2,1)S(1)} %collective-permute-done.1.refs_0_.odd_ref, bf16[4,1,2,64,256]{4,3,2,1,0:T(8,128)(2,1)S(1)} %collective-permute-done.2.refs_1_.odd_ref, ...), custom_call_target="tpu_custom_call" | custom-call | flops 805306368 | bytes 5505024 | tf_op jit(solution)/shard_map/pallas_call | solution.py:24
  29.2 1.9 %collective-permute-done.odd_ref.part_ref = bf16[4,1,2,64,256]{4,3,2,1,0:T(8,128)(2,1)S(1)} collective-permute-done((bf16[4,1,2,64,256]{4,3,2,1,0:T(8,128)(2,1)S(1)}, bf16[4,1,2,64,256]{4,3,2,1,0:T(8,128)(2,1)S(1)}, u32[]{:S(2)}, u32[]{:S(2)}) %collective-permute-start) | collective-permute-done | bytes 262176 | tf_op jit(solution)/shard_map/ppermute | solution.py:19
  31.1 1.7 %collective-permute-start.4 = (bf16[1,1,2,64,256]{4,3,2,1,0:T(8,128)(2,1)S(1)}, bf16[1,1,2,64,256]{4,3,2,1,0:T(8,128)(2,1)S(1)}, u32[]{:S(2)}, u32[]{:S(2)}) collective-permute-start(bf16[1,1,2,64,256]{4,3,2,1,0:T(8,128)(2,1)S(1)} %shard_map.31), channel_id=1, source_target_pairs={{0,2},{2,0},{4,6},{6,4},{8,10},{10,8},{12,14},{14,12},{16,18},{18,... | collective-permute-start | bytes 196616 | tf_op jit(solution)/shard_map/ppermute | solution.py:19
  32.8 0.5 %shard_map.39.second_ref = f32[4,12]{1,0:T(4,128)S(1)} custom-call(bf16[12,1,2,64,1024]{4,3,2,1,0:T(8,128)(2,1)S(1)} %copy-done, bf16[4,1,2,64,256]{4,3,2,1,0:T(8,128)(2,1)S(1)} %collective-permute-done.odd_ref.part_ref, f32[1,2,768,256]{3,2,1,0:T(8,128)S(1)} %shard_map.30.refs_0_.grams_ref), custom_call_target="tpu_custom_call" | custom-call | flops 201326592 | bytes 4980928 | tf_op jit(solution)/shard_map/pallas_call | solution.py:24
  33.3 0.0 collective-permute-done.8.refs_0_
  33.3 0.0 collective-permute-done.9.refs_1_
  33.4 0.6 %shard_map.35.refs_0_.grams_ref = f32[1,2,768,256]{3,2,1,0:T(8,128)S(1)} custom-call(bf16[12,1,2,64,1024]{4,3,2,1,0:T(8,128)(2,1)S(1)} %copy-done, bf16[4,1,2,64,256]{4,3,2,1,0:T(8,128)(2,1)S(1)} %collective-permute-done.8.refs_0_, bf16[4,1,2,64,256]{4,3,2,1,0:T(8,128)(2,1)S(1)} %collective-permute-done.9.refs_1_), custom_call_target="tpu_custom_call" | custom-call | flops 402653184 | bytes 5242880 | tf_op jit(solution)/shard_map/pallas_call | solution.py:24
  34.0 0.5 %collective-permute-done.7.even_ref = bf16[3,1,2,64,256]{4,3,2,1,0:T(8,128)(2,1)S(1)} collective-permute-done((bf16[3,1,2,64,256]{4,3,2,1,0:T(8,128)(2,1)S(1)}, bf16[3,1,2,64,256]{4,3,2,1,0:T(8,128)(2,1)S(1)}, u32[]{:S(2)}, u32[]{:S(2)}) %collective-permute-start.7) | collective-permute-done | bytes 196640 | tf_op jit(solution)/shard_map/ppermute | solution.py:19
  34.5 0.0 collective-permute-done.5.part_ref
  34.5 0.8 %shard_map.37 = (f32[1,2,768,64]{3,2,1,0:T(8,128)S(1)}, f32[3,12]{1,0:T(4,128)S(1)}) custom-call(bf16[12,1,2,64,1024]{4,3,2,1,0:T(8,128)(2,1)S(1)} %copy-done, bf16[4,1,2,64,256]{4,3,2,1,0:T(8,128)(2,1)S(1)} %collective-permute-done.5.part_ref, bf16[3,1,2,64,256]{4,3,2,1,0:T(8,128)(2,1)S(1)} %shard_map.36.last_ref, ...), custom_call_target="tpu_custom_call" | custom-call | flops 201326592 | bytes 5570704 | tf_op jit(solution)/shard_map/pallas_call | solution.py:24
  35.3 0.1 collective-permute-done.4.end_ref
  35.4 0.5 %shard_map.40.a_ref = f32[3,4,12]{2,1,0:T(4,128)S(1)} custom-call(bf16[12,1,2,64,1024]{4,3,2,1,0:T(8,128)(2,1)S(1)} %copy-done, bf16[1,1,2,64,256]{4,3,2,1,0:T(8,128)(2,1)S(1)} %collective-permute-done.4.end_ref, f32[1,2,768,64]{3,2,1,0:T(8,128)S(1)} %get-tuple-element.13.ends_ref, f32[4,12]{1,0:T(4,128)S(1)} %shard_map.38.own_ref, ...), custom_call_target="tpu_custom_call" | custom-call | flops 50331648 | bytes 3605584 | tf_op jit(solution)/shard_map/pallas_call | solution.py:24
  35.9 0.0 collective-permute-start.10
  35.9 1.2 %collective-permute-done.10.b_ref = f32[3,4,12]{2,1,0:T(4,128)S(1)} collective-permute-done((f32[3,4,12]{2,1,0:T(4,128)S(1)}, f32[3,4,12]{2,1,0:T(4,128)S(1)}, u32[]{:S(2)}, u32[]{:S(2)}) %collective-permute-start.10) | collective-permute-done | bytes 608 | tf_op jit(solution)/shard_map/ppermute | solution.py:19
  37.0 0.6 %shard_map.41 = f32[3,4,12]{2,1,0:T(4,128)} custom-call(f32[3,4,12]{2,1,0:T(4,128)S(1)} %shard_map.40.a_ref, f32[3,4,12]{2,1,0:T(4,128)S(1)} %collective-permute-done.10.b_ref), custom_call_target="tpu_custom_call" | custom-call | bytes 1728 | tf_op jit(solution)/shard_map/pallas_call | solution.py:24
  (6 shorter events, 0.1 us)
Async XLA Ops:
  0.0 4.1 %copy-start.1 = (bf16[4,1,2,64,1024]{4,3,2,1,0:T(8,128)(2,1)S(1)}, bf16[4,1,2,64,1024]{4,3,2,1,0:T(8,128)(2,1)}, u32[]{:S(2)}) copy-start(bf16[4,1,2,64,1024]{4,3,2,1,0:T(8,128)(2,1)} %val_ref.3) | copy-start | bytes 3145732
  1.1 13.2 %collective-permute-start.1 = (bf16[4,1,2,64,256]{4,3,2,1,0:T(8,128)(2,1)S(1)}, bf16[4,1,2,64,256]{4,3,2,1,0:T(8,128)(2,1)S(1)}, u32[]{:S(2)}, u32[]{:S(2)}) collective-permute-start(bf16[4,1,2,64,256]{4,3,2,1,0:T(8,128)(2,1)S(1)} %shard_map.29.even_ref.refs_0_), channel_id=1, source_target_pairs={{0,4},{2,6},{4,8},{6,10},{8,12},{10,14},{12,16},{14,18},{16,20},{1... | collective-permute-start | bytes 786440 | tf_op jit(solution)/shard_map/ppermute | solution.py:19
  4.1 23.2 %copy-start = (bf16[12,1,2,64,1024]{4,3,2,1,0:T(8,128)(2,1)S(1)}, bf16[12,1,2,64,1024]{4,3,2,1,0:T(8,128)(2,1)}, u32[]{:S(2)}) copy-start(bf16[12,1,2,64,1024]{4,3,2,1,0:T(8,128)(2,1)} %train_ref.11) | copy-start | bytes 9437188
  4.2 15.7 %collective-permute-start.2 = (bf16[4,1,2,64,256]{4,3,2,1,0:T(8,128)(2,1)S(1)}, bf16[4,1,2,64,256]{4,3,2,1,0:T(8,128)(2,1)S(1)}, u32[]{:S(2)}, u32[]{:S(2)}) collective-permute-start(bf16[4,1,2,64,256]{4,3,2,1,0:T(8,128)(2,1)S(1)} %get-tuple-element.11.even_ref.refs_1_), channel_id=1, source_target_pairs={{0,4},{2,6},{4,8},{6,10},{8,12},{10,14},{12,16},{14,18},{16,20},{1... | collective-permute-start | bytes 786440 | tf_op jit(solution)/shard_map/ppermute | solution.py:19
  5.8 10.3 %collective-permute-start.6 = (bf16[3,1,2,64,256]{4,3,2,1,0:T(8,128)(2,1)S(1)}, bf16[3,1,2,64,256]{4,3,2,1,0:T(8,128)(2,1)S(1)}, u32[]{:S(2)}, u32[]{:S(2)}) collective-permute-start(bf16[3,1,2,64,256]{4,3,2,1,0:T(8,128)(2,1)S(1)} %slice.3), channel_id=1, source_target_pairs={{0,2},{2,0},{4,6},{6,4},{8,10},{10,8},{12,14},{14,12},{16,18},{18,... | collective-permute-start | bytes 589832 | tf_op jit(solution)/shard_map/ppermute | solution.py:19
  7.3 18.2 %collective-permute-start.3 = (bf16[4,1,2,64,256]{4,3,2,1,0:T(8,128)(2,1)S(1)}, bf16[4,1,2,64,256]{4,3,2,1,0:T(8,128)(2,1)S(1)}, u32[]{:S(2)}, u32[]{:S(2)}) collective-permute-start(bf16[4,1,2,64,256]{4,3,2,1,0:T(8,128)(2,1)S(1)} %get-tuple-element.12.even_ref.refs_2_), channel_id=1, source_target_pairs={{0,4},{2,6},{4,8},{6,10},{8,12},{10,14},{12,16},{14,18},{16,20},{1... | collective-permute-start | bytes 786440 | tf_op jit(solution)/shard_map/ppermute | solution.py:19
  8.8 22.3 %collective-permute-start = (bf16[4,1,2,64,256]{4,3,2,1,0:T(8,128)(2,1)S(1)}, bf16[4,1,2,64,256]{4,3,2,1,0:T(8,128)(2,1)S(1)}, u32[]{:S(2)}, u32[]{:S(2)}) collective-permute-start(bf16[4,1,2,64,256]{4,3,2,1,0:T(8,128)(2,1)S(1)} %get-tuple-element.10.even_ref.refs_3_), channel_id=1, source_target_pairs={{0,4},{2,6},{4,8},{6,10},{8,12},{10,14},{12,16},{14,18},{16,20},{1... | collective-permute-start | bytes 786440 | tf_op jit(solution)/shard_map/ppermute | solution.py:19
  14.3 19.0 %collective-permute-start.8 = (bf16[4,1,2,64,256]{4,3,2,1,0:T(8,128)(2,1)S(1)}, bf16[4,1,2,64,256]{4,3,2,1,0:T(8,128)(2,1)S(1)}, u32[]{:S(2)}, u32[]{:S(2)}) collective-permute-start(bf16[4,1,2,64,256]{4,3,2,1,0:T(8,128)(2,1)S(1)} %shard_map.33), channel_id=1, source_target_pairs={{0,2},{2,0},{4,6},{6,4},{8,10},{10,8},{12,14},{14,12},{16,18},{18,... | collective-permute-start | bytes 786440 | tf_op jit(solution)/shard_map/ppermute | solution.py:19
  19.9 13.4 %collective-permute-start.9 = (bf16[4,1,2,64,256]{4,3,2,1,0:T(8,128)(2,1)S(1)}, bf16[4,1,2,64,256]{4,3,2,1,0:T(8,128)(2,1)S(1)}, u32[]{:S(2)}, u32[]{:S(2)}) collective-permute-start(bf16[4,1,2,64,256]{4,3,2,1,0:T(8,128)(2,1)S(1)} %shard_map.34), channel_id=1, source_target_pairs={{0,2},{2,0},{4,6},{6,4},{8,10},{10,8},{12,14},{14,12},{16,18},{18,... | collective-permute-start | bytes 786440 | tf_op jit(solution)/shard_map/ppermute | solution.py:19
  21.6 12.9 %collective-permute-start.7 = (bf16[3,1,2,64,256]{4,3,2,1,0:T(8,128)(2,1)S(1)}, bf16[3,1,2,64,256]{4,3,2,1,0:T(8,128)(2,1)S(1)}, u32[]{:S(2)}, u32[]{:S(2)}) collective-permute-start(bf16[3,1,2,64,256]{4,3,2,1,0:T(8,128)(2,1)S(1)} %collective-permute-done.6.refs_0_.odd_ref), channel_id=1, source_target_pairs={{0,4},{2,6},{4,8},{6,10},{8,12},{10,14},{12,16},{14,18},{16,20},{1... | collective-permute-start | bytes 589832 | tf_op jit(solution)/shard_map/ppermute | solution.py:19
  25.5 9.0 %collective-permute-start.5 = (bf16[4,1,2,64,256]{4,3,2,1,0:T(8,128)(2,1)S(1)}, bf16[4,1,2,64,256]{4,3,2,1,0:T(8,128)(2,1)S(1)}, u32[]{:S(2)}, u32[]{:S(2)}) collective-permute-start(bf16[4,1,2,64,256]{4,3,2,1,0:T(8,128)(2,1)S(1)} %shard_map.32), channel_id=1, source_target_pairs={{0,2},{2,0},{4,6},{6,4},{8,10},{10,8},{12,14},{14,12},{16,18},{18,... | collective-permute-start | bytes 786440 | tf_op jit(solution)/shard_map/ppermute | solution.py:19
  31.1 4.3 %collective-permute-start.4 = (bf16[1,1,2,64,256]{4,3,2,1,0:T(8,128)(2,1)S(1)}, bf16[1,1,2,64,256]{4,3,2,1,0:T(8,128)(2,1)S(1)}, u32[]{:S(2)}, u32[]{:S(2)}) collective-permute-start(bf16[1,1,2,64,256]{4,3,2,1,0:T(8,128)(2,1)S(1)} %shard_map.31), channel_id=1, source_target_pairs={{0,2},{2,0},{4,6},{6,4},{8,10},{10,8},{12,14},{14,12},{16,18},{18,... | collective-permute-start | bytes 196616 | tf_op jit(solution)/shard_map/ppermute | solution.py:19
  35.9 1.2 %collective-permute-start.10 = (f32[3,4,12]{2,1,0:T(4,128)S(1)}, f32[3,4,12]{2,1,0:T(4,128)S(1)}, u32[]{:S(2)}, u32[]{:S(2)}) collective-permute-start(f32[3,4,12]{2,1,0:T(4,128)S(1)} %shard_map.40.a_ref), channel_id=1, source_target_pairs={{0,1},{1,0},{2,3},{3,2},{4,5},{5,4},{6,7},{7,6},{8,9},{9,8},{10,11... | collective-permute-start | bytes 1736 | tf_op jit(solution)/shard_map/ppermute | solution.py:19
